TPU v7x, 32 devices: a whole 2x2x4 slice. The times are simulated.
32 devices in a mesh: groups: 2 (over y), seq: 4 (over z), mp: 2 (over x), pipe: 2 (over core).
Axes of the slice: x: 2, y: 2, z: 4, core: 2. Of those that a mesh axis runs over, the one named last changes fastest.
Arguments:
- query: bfloat16 [16384, 1024], P(('groups', 'seq', 'pipe'), 'mp'), parts along dimension 0, may hold values from -6 to 6
- key_in: bfloat16 [16384, 1024], P(('groups', 'seq', 'pipe'), 'mp'), parts along dimension 0, may hold values from -6 to 6
- value_in: bfloat16 [16384, 1024], P(('groups', 'seq', 'pipe'), 'mp'), parts along dimension 0, may hold values from -6 to 6
- gate_u: bfloat16 [16384, 1024], P(('groups', 'seq', 'pipe'), 'mp'), parts along dimension 0, may hold values from -6 to 6
- grad_out: bfloat16 [16384, 1024], P(('groups', 'seq', 'pipe'), 'mp'), parts along dimension 0, may hold values from -6 to 6
- segment_ids: int32 [16384], P('groups'), parts along dimension 0, may hold values from 0 to 95, never falling along the last dimension, each value on 1 to 256 neighbouring positions
- sample_slot: int32 [16384], P(('groups', 'seq', 'pipe')), parts along dimension 0, may hold values from -1 to 511, as said below
- owned_input: bfloat16 [8192, 1024], P(('groups', 'seq')), parts along dimension 0, may hold values from -6 to 6
- task_grad: float32 [8192, 4], P(('groups', 'seq')), parts along dimension 0, may hold values from -6 to 6
- w_in: bfloat16 [4, 1024, 512], P(('mp', 'pipe')), may hold values from -0.1875 to 0.1875
- w_out: bfloat16 [4, 512, 256], P(('mp', 'pipe')), may hold values from -0.25 to 0.25
- w_gate: bfloat16 [4, 1024, 4], P(('mp', 'pipe')), may hold values from -0.1875 to 0.1875
- tower: bfloat16 [4, 256], replicated, may hold values from -6 to 6
Outputs:
- grad_q: bfloat16 [16384, 1024], P(('groups', 'seq', 'pipe'), 'mp'), parts along dimension 0
- grad_k: bfloat16 [16384, 1024], P(('groups', 'seq', 'pipe'), 'mp'), parts along dimension 0
- grad_v: bfloat16 [16384, 1024], P(('groups', 'seq', 'pipe'), 'mp'), parts along dimension 0
- grad_u: bfloat16 [16384, 1024], P(('groups', 'seq', 'pipe'), 'mp'), parts along dimension 0
There are 2 independent parts, one for each index of `groups`. A program takes and returns all parts, laid end to end along the dimension named above; an argument that names none is the same for every part. Nothing has to cross between parts.
Inputs may be any that keep to these rules, and one draw needn't show every extreme that they name: `segment_ids`: A user's events are consecutive rows: the ids never fall along the rows, every user has at most 256 events and some user exactly 256. `sample_slot`: rows whose value is -1 carry no sample. Within one block of 1024 rows no value other than -1 appears twice. In every draw some owner receives all 128 slots from every block.
All inputs are finite; a program needn't handle non-finite values.
Results may differ from a plain program's by a relative error of at most 0.0062.
Values may be sent and summed in bfloat16 or wider, within the bound.
A program may use at most 128 MiB of HBM per device.

v0:
```python
import math

import jax
import jax.numpy as jnp
from jax import lax
from jax.sharding import PartitionSpec as P

HDIM = 128
MOST = 256


def shifted(block, axis, distance):
    devices = range(lax.axis_size(axis))
    route = [(i - distance, i) for i in devices if i - distance in devices]
    return lax.ppermute(block, axis, route)


def silu_slope(inputs, logistic):
    return logistic * (1.0 + inputs * (1.0 - logistic))


def expert_backward(owned_input, task_grad, w_in, w_out, w_gate, tower):
    n_local = w_in.shape[0]
    n_model = lax.axis_size("mp")
    n_pipe = lax.axis_size("pipe")
    features = w_in.shape[1] // n_model
    hidden_width = w_in.shape[2]
    n_tasks = w_gate.shape[2]
    block_rows = owned_input.shape[0] // n_pipe
    pre_act = jnp.einsum("rd,edh->erh", owned_input, w_in, preferred_element_type=jnp.float32)
    logistic = jax.nn.sigmoid(pre_act)
    activation = (pre_act * logistic).astype(jnp.bfloat16)
    expert_out = jnp.einsum("erh,eho->ero", activation, w_out, preferred_element_type=jnp.float32)
    gate_prob = jax.nn.sigmoid(
        jnp.einsum("rd,edt->ert", owned_input, w_gate, preferred_element_type=jnp.float32)
    )
    towers = tower.astype(jnp.float32)
    task_score = jnp.sum(expert_out[:, :, None, :] * towers[None, None, :, :], axis=3)
    weighted = task_grad[None, :, :] * gate_prob
    grad_hidden = jnp.sum(weighted[:, :, :, None] * towers[None, None, :, :], axis=2).astype(
        jnp.bfloat16
    )
    grad_act = jnp.einsum("ero,eho->erh", grad_hidden, w_out, preferred_element_type=jnp.float32)
    grad_pre = (grad_act * silu_slope(pre_act, logistic)).astype(jnp.bfloat16)
    grad_logit = (task_grad[None, :, :] * task_score * gate_prob * (1.0 - gate_prob)).astype(
        jnp.bfloat16
    )
    pre_blocks = grad_pre.reshape(n_local, n_pipe, block_rows, hidden_width)
    logit_blocks = grad_logit.reshape(n_local, n_pipe, block_rows, n_tasks)
    in_blocks = w_in.reshape(n_local, n_model, features, hidden_width)
    gate_blocks = w_gate.reshape(n_local, n_model, features, n_tasks)
    n_pieces = block_rows * lax.axis_size(("mp", "pipe")) // block_rows
    piece_index = jnp.arange(n_pieces, dtype=jnp.int32)
    model_index = piece_index // n_pipe
    pipe_index = piece_index % n_pipe
    term_sum = jnp.einsum(
        "ebrh,ebfh->brf",
        jnp.take(pre_blocks, pipe_index, axis=1),
        jnp.take(in_blocks, model_index, axis=1),
        preferred_element_type=jnp.float32,
    )
    term_sum = term_sum + jnp.einsum(
        "ebrt,ebft->brf",
        jnp.take(logit_blocks, pipe_index, axis=1),
        jnp.take(gate_blocks, model_index, axis=1),
        preferred_element_type=jnp.float32,
    )
    summed = lax.psum_scatter(
        term_sum.reshape(block_rows * lax.axis_size(("mp", "pipe")), features),
        ("mp", "pipe"),
        scatter_dimension=0,
        tiled=True,
    )
    return summed.astype(jnp.bfloat16)


def head_major(rows_array, local_heads):
    n_rows = rows_array.shape[0]
    return rows_array.reshape(n_rows, local_heads, HDIM).transpose(1, 0, 2)


def row_major(heads_array):
    n_heads = heads_array.shape[0]
    n_rows = heads_array.shape[1]
    return heads_array.transpose(1, 0, 2).reshape(n_rows, n_heads * HDIM)


def shards(
    query,
    key_in,
    value_in,
    gate_u,
    grad_out,
    segment_ids,
    sample_slot,
    owned_input,
    task_grad,
    w_in,
    w_out,
    w_gate,
    tower,
):
    tok_rows = query.shape[0]
    feat_cols = query.shape[1]
    local_heads = feat_cols // HDIM
    owners = lax.axis_size("seq")
    slot_count = owned_input.shape[0] // lax.axis_size("pipe") // owners
    expert_grad = expert_backward(owned_input, task_grad, w_in, w_out, w_gate, tower)
    returned = lax.all_to_all(
        expert_grad.reshape(owners, slot_count, feat_cols),
        "seq",
        split_axis=0,
        concat_axis=0,
        tiled=True,
    )
    flat_rows = returned.reshape(owners * slot_count, feat_cols)
    picked = jnp.take(flat_rows, jnp.maximum(sample_slot, 0), axis=0).astype(jnp.float32)
    upstream = grad_out.astype(jnp.float32) + jnp.where(sample_slot[:, None] >= 0, picked, 0.0)
    position = lax.axis_index(("seq", "pipe"))
    seg_here = lax.dynamic_slice_in_dim(segment_ids, position * tok_rows, tok_rows)
    seg_prev = lax.dynamic_slice_in_dim(
        segment_ids, jnp.maximum(position * tok_rows - tok_rows, 0), tok_rows
    )
    seg_prev = jnp.where(position > 0, seg_prev, -1)
    key_prev, value_prev = shifted((key_in, value_in), ("seq", "pipe"), 1)
    key_count = tok_rows + tok_rows
    key_heads = head_major(jnp.concatenate([key_prev, key_in], axis=0), local_heads)
    value_heads = head_major(jnp.concatenate([value_prev, value_in], axis=0), local_heads)
    seg_keys = jnp.concatenate([seg_prev, seg_here], axis=0)
    key_pos = jnp.arange(key_count, dtype=jnp.int32) - tok_rows
    query_pos = jnp.arange(tok_rows, dtype=jnp.int32)
    query_heads = head_major(query, local_heads)
    u_heads = head_major(gate_u, local_heads)
    upstream_heads = head_major(upstream, local_heads)
    score_scale = 1.0 / math.sqrt(HDIM)
    weight_norm = 1.0 / math.sqrt(MOST)
    grad_keys = jnp.zeros((local_heads, key_count, HDIM), jnp.float32)
    grad_values = jnp.zeros((local_heads, key_count, HDIM), jnp.float32)
    query_span = min(tok_rows, 512)
    grad_q_parts = []
    grad_u_parts = []
    for block_index in range(tok_rows // query_span):
        low_q = block_index * query_span
        high_q = low_q + query_span
        high_k = tok_rows + high_q
        low_k = max(0, tok_rows + low_q - MOST + 1)
        q_part = query_heads[:, low_q:high_q]
        k_part = key_heads[:, low_k:high_k]
        v_part = value_heads[:, low_k:high_k]
        scores = (
            jnp.einsum("hqd,hkd->hqk", q_part, k_part, preferred_element_type=jnp.float32)
            * score_scale
        )
        visible = (seg_here[low_q:high_q, None] == seg_keys[None, low_k:high_k]) & (
            key_pos[None, low_k:high_k] <= query_pos[low_q:high_q, None]
        )
        logistic = jax.nn.sigmoid(scores)
        weights = (jnp.where(visible[None], scores * logistic, 0.0) * weight_norm).astype(
            jnp.bfloat16
        )
        attended = jnp.einsum("hqk,hkd->hqd", weights, v_part, preferred_element_type=jnp.float32)
        grad_here = upstream_heads[:, low_q:high_q]
        grad_u_parts.append((grad_here * attended).astype(jnp.bfloat16))
        grad_attn = (grad_here * u_heads[:, low_q:high_q].astype(jnp.float32)).astype(jnp.bfloat16)
        value_term = jnp.einsum(
            "hqk,hqd->hkd", weights, grad_attn, preferred_element_type=jnp.float32
        )
        grad_values = lax.dynamic_update_slice_in_dim(
            grad_values, grad_values[:, low_k:high_k] + value_term, low_k, 1
        )
        grad_weights = jnp.einsum(
            "hqd,hkd->hqk", grad_attn, v_part, preferred_element_type=jnp.float32
        )
        grad_scores = (
            jnp.where(visible[None], grad_weights * silu_slope(scores, logistic), 0.0)
            * (score_scale * weight_norm)
        ).astype(jnp.bfloat16)
        grad_q_parts.append(
            jnp.einsum(
                "hqk,hkd->hqd", grad_scores, k_part, preferred_element_type=jnp.float32
            ).astype(jnp.bfloat16)
        )
        key_term = jnp.einsum(
            "hqk,hqd->hkd", grad_scores, q_part, preferred_element_type=jnp.float32
        )
        grad_keys = lax.dynamic_update_slice_in_dim(
            grad_keys, grad_keys[:, low_k:high_k] + key_term, low_k, 1
        )
    lent_keys = row_major(grad_keys[:, :tok_rows])
    lent_values = row_major(grad_values[:, :tok_rows])
    back_keys, back_values = shifted((lent_keys, lent_values), ("seq", "pipe"), -1)
    own_keys = row_major(grad_keys[:, tok_rows:])
    own_values = row_major(grad_values[:, tok_rows:])
    cut_row = tok_rows - tok_rows
    own_keys = jnp.concatenate([own_keys[:cut_row], own_keys + back_keys], axis=0)
    own_values = jnp.concatenate([own_values[:cut_row], own_values + back_values], axis=0)
    grad_q = row_major(jnp.concatenate(grad_q_parts, axis=1))
    grad_u = row_major(jnp.concatenate(grad_u_parts, axis=1))
    return (grad_q, own_keys.astype(jnp.bfloat16), own_values.astype(jnp.bfloat16), grad_u)


def solution(mesh):
    return jax.shard_map(
        shards,
        mesh=mesh,
        in_specs=(
            P(("groups", "seq", "pipe"), "mp"),
            P(("groups", "seq", "pipe"), "mp"),
            P(("groups", "seq", "pipe"), "mp"),
            P(("groups", "seq", "pipe"), "mp"),
            P(("groups", "seq", "pipe"), "mp"),
            P("groups"),
            P(("groups", "seq", "pipe")),
            P(("groups", "seq"), None),
            P(("groups", "seq"), None),
            P(("mp", "pipe"), None, None),
            P(("mp", "pipe"), None, None),
            P(("mp", "pipe"), None, None),
            P(),
        ),
        out_specs=(
            P(("groups", "seq", "pipe"), "mp"),
            P(("groups", "seq", "pipe"), "mp"),
            P(("groups", "seq", "pipe"), "mp"),
            P(("groups", "seq", "pipe"), "mp"),
        ),
        check_vma=False,
    )
```

profile of v0, /device:TPU:1, one launch (start us, length us, event | category | flops | bytes accessed | tf_op | source)
XLA Modules:
  0.0 209.2 jit_solution(1237353378336898367)
XLA Ops:
  20.8 3.6 %fusion.24 = f32[4,512,512]{2,1,0:T(8,128)S(1)} fusion(bf16[4,512,512]{2,1,0:T(8,128)(2,1)} %gather_fusion.2, bf16[4,512,512]{2,1,0:T(8,128)(2,1)} %gather_fusion.1, pred[4]{0:T(512)(128)(4,1)S(1)} %get-tuple-element.36, pred[4]{0:T(512)(128)(4,1)S(1)} %get-tuple-element.37), kind=kOutput, calls=%fused_computation.40 | convolution fusion | flops 1075838976 | bytes 8388616 | tf_op jit(solution)/shard_map/ebrh,ebfh->brf/dot_general | solution.py:56
  24.4 3.0 %convolution_add_fusion = f32[4,512,512]{2,1,0:T(8,128)} fusion(f32[4,512,512]{2,1,0:T(8,128)S(1)} %fusion.24, bf16[4,512,4]{1,2,0:T(4,128)(2,1)S(1)} %gather_fusion.4, bf16[4,512,4]{1,2,0:T(4,128)(2,1)S(1)} %gather_fusion.3, pred[4]{0:T(512)(128)(4,1)S(1)} %get-tuple-element.36, pred[4]{0:T(512)(128)(4,1)S(1)} %get-tuple-element.37), kind=kOutput, calls=%fused_computation.37 | convolution fusion | flops 9453568 | bytes 8421384 | tf_op jit(solution)/shard_map/ebrt,ebft->brf/dot_general | solution.py:62
  29.2 4.6 %collective-permute-start.1 = (bf16[1024,512]{0,1:T(8,128)(2,1)S(1)}, bf16[1024,512]{0,1:T(8,128)(2,1)}, u32[]{:S(2)}, u32[]{:S(2)}) collective-permute-start(bf16[1024,512]{0,1:T(8,128)(2,1)S(1)} %copy.67), channel_id=1, source_target_pairs={{0,1},{1,4},{4,5},{5,8},{8,9},{9,12},{12,13},{2,3},{3,6},{6,7},{7,... | collective-permute-start | bytes 3145736 | tf_op jit(solution)/shard_map/ppermute | solution.py:15
  51.6 5.1 %collective-permute-done = bf16[1024,512]{0,1:T(8,128)(2,1)} collective-permute-done((bf16[1024,512]{0,1:T(8,128)(2,1)S(1)}, bf16[1024,512]{0,1:T(8,128)(2,1)}, u32[]{:S(2)}, u32[]{:S(2)}) %collective-permute-start) | collective-permute-done | bytes 1048608 | tf_op jit(solution)/shard_map/ppermute | solution.py:15
  60.7 6.3 %fusion.11 = (bf16[4,512,767]{2,1,0:T(8,128)(2,1)}, f32[4,767,512]{1,2,0:T(8,128)}) fusion(pred[512,767]{1,0:T(8,128)(4,1)} %get-tuple-element.34, bf16[4,1024,128]{2,1,0:T(8,128)(2,1)S(1)} %bitcast.234, bf16[4,2048,128]{2,1,0:T(8,128)(2,1)} %bitcast.246), kind=kOutput, calls=%fused_computation.19 | convolution fusion | flops 414695424 | bytes 11128832 | tf_op jit(solution)/shard_map/hqd,hkd->hqk/dot_general | solution.py:151
  67.0 7.7 %reduce-scatter.2.cloned.1.call-done = f32[512,512]{1,0:T(8,128)} async-done(((f32[2048,512]{1,0:T(8,128)}), f32[512,512]{1,0:T(8,128)}) %reduce-scatter.2.cloned.1.call-update) | async-done | bytes 1048592 | tf_op jit(solution)/shard_map/reduce_scatter | solution.py:68
  76.7 4.3 %all-to-all-start = ((bf16[4,128,512]{2,1,0:T(8,128)(2,1)}), bf16[4,128,512]{2,1,0:T(8,128)(2,1)S(1)}, u32[]{:S(2)}, u32[]{:S(2)}) async-start(bf16[4,128,512]{2,1,0:T(8,128)(2,1)} %bitcast.31), calls=%async_computation.1 | async-start | bytes 1048576 | tf_op jit(solution)/shard_map/all_to_all | solution.py:109
  81.0 6.3 %fusion.23 = (bf16[4,512,767]{2,1,0:T(8,128)(2,1)}, f32[4,767,512]{1,2,0:T(8,128)}) fusion(pred[512,767]{1,0:T(8,128)(4,1)S(1)} %get-tuple-element.35, bf16[4,1024,128]{2,1,0:T(8,128)(2,1)S(1)} %bitcast.235, bf16[4,2048,128]{2,1,0:T(8,128)(2,1)} %bitcast.247), kind=kOutput, calls=%fused_computation.34 | convolution fusion | flops 414695424 | bytes 11128832 | tf_op jit(solution)/shard_map/hqd,hkd->hqk/dot_general | solution.py:151
  87.3 7.7 %all-to-all-done = bf16[4,128,512]{2,1,0:T(8,128)(2,1)S(1)} async-done(((bf16[4,128,512]{2,1,0:T(8,128)(2,1)}), bf16[4,128,512]{2,1,0:T(8,128)(2,1)S(1)}, u32[]{:S(2)}, u32[]{:S(2)}) %all-to-all-start) | async-done | bytes 524320 | tf_op jit(solution)/shard_map/all_to_all | solution.py:109
  95.0 4.0 %gather_fusion = bf16[1024,512]{1,0:T(8,128)(2,1)S(1)} fusion(bf16[512,512]{1,0:T(8,128)(2,1)S(1)} %bitcast.211, s32[1024]{0:T(1024)S(1)} %maximum_clamp_fusion), kind=kCustom, calls=%fused_computation.4 | custom fusion | bytes 2101248 | tf_op jit(solution)/shard_map/jit(_take)/gather | solution.py:117
  104.9 6.9 %fusion.8 = bf16[4,512,767]{2,1,0:T(8,128)(2,1)S(1)} fusion(f32[4,767,512]{1,2,0:T(8,128)} %get-tuple-element.33, pred[512,767]{1,0:T(8,128)(4,1)} %get-tuple-element.34, bf16[4,2048,128]{2,1,0:T(8,128)(2,1)} %bitcast.242, f32[4,1024,128]{2,1,0:T(8,128)S(1)} %bitcast.215, bf16[4,1024,128]{2,1,0:T(8,128)(2,1)S(1)} %bitcast.238), kind=kOutput, calls=%fused_computation.16 | convolution fusion | flops 421765120 | bytes 12185600 | tf_op jit(solution)/shard_map/hqd,hkd->hqk/dot_general | solution.py:171
  111.8 7.2 %fusion.20 = bf16[4,512,767]{2,1,0:T(8,128)(2,1)S(1)} fusion(f32[4,767,512]{1,2,0:T(8,128)} %get-tuple-element.31, pred[512,767]{1,0:T(8,128)(4,1)S(1)} %get-tuple-element.35, bf16[4,2048,128]{2,1,0:T(8,128)(2,1)} %bitcast.243, f32[4,1024,128]{2,1,0:T(8,128)S(1)} %bitcast.216, bf16[4,1024,128]{2,1,0:T(8,128)(2,1)S(1)} %bitcast.239), kind=kOutput, calls=%fused_computation.31 | convolution fusion | flops 421765120 | bytes 12185600 | tf_op jit(solution)/shard_map/hqd,hkd->hqk/dot_general | solution.py:171
  125.3 11.0 %dynamic_update_slice.13 = f32[4,2048,128]{1,2,0:T(8,128)} dynamic-update-slice(f32[4,2048,128]{1,2,0:T(8,128)} %dynamic_update_slice.12, f32[4,767,128]{1,2,0:T(8,128)} %slice_add_fusion.1, s32[]{:T(128)} %constant.90.clone.1, s32[]{:T(128)} %constant.101.clone.1, s32[]{:T(128)} %constant.90.clone.1) | dynamic-update-slice | bytes 3141636 | tf_op jit(solution)/shard_map/dynamic_update_slice | solution.py:186
  136.3 4.2 %fusion.81 = (f32[4,1024,128]{1,2,0:T(8,128)S(1)}, f32[4,1024,128]{1,2,0:T(8,128)}) fusion(f32[4,2048,128]{1,2,0:T(8,128)} %dynamic_update_slice.13), kind=kLoop, calls=%fused_computation.138 | loop fusion | bytes 8388608 | tf_op jit(solution)/shard_map/slice | solution.py:189
  142.3 3.6 %collective-permute-start.2 = (f32[1024,512]{1,0:T(8,128)}, f32[1024,512]{1,0:T(8,128)}, u32[]{:S(2)}, u32[]{:S(2)}) collective-permute-start(f32[1024,512]{1,0:T(8,128)} %copy.77), channel_id=1, source_target_pairs={{1,0},{4,1},{5,4},{8,5},{9,8},{12,9},{13,12},{3,2},{6,3},{7,6},{10... | collective-permute-start | bytes 6291464 | tf_op jit(solution)/shard_map/ppermute | solution.py:15
  145.9 2.8 %fusion.79 = f32[4,767,128]{1,2,0:T(8,128)S(1)} fusion(bf16[4,512,767]{2,1,0:T(8,128)(2,1)} %get-tuple-element.30, f32[4,1024,128]{2,1,0:T(8,128)} %bitcast.217, bf16[4,1024,128]{2,1,0:T(8,128)(2,1)S(1)} %bitcast.240), kind=kOutput, calls=%fused_computation.136 | convolution fusion | flops 402915328 | bytes 6289408 | tf_op jit(solution)/shard_map/hqk,hqd->hkd/dot_general | solution.py:165
  148.8 2.9 %dynamic_update_slice.14 = f32[4,2048,128]{1,2,0:T(8,128)} pad(f32[4,767,128]{1,2,0:T(8,128)S(1)} %fusion.79, f32[]{:T(128)} %constant.96.clone.1), padding=0_0x769_512x0_0 | pad | bytes 5765124 | tf_op jit(solution)/shard_map/dynamic_update_slice | solution.py:168
  154.6 11.0 %dynamic_update_slice.15 = f32[4,2048,128]{1,2,0:T(8,128)} dynamic-update-slice(f32[4,2048,128]{1,2,0:T(8,128)} %dynamic_update_slice.14, f32[4,767,128]{1,2,0:T(8,128)} %slice_add_fusion, s32[]{:T(128)} %constant.90.clone.1, s32[]{:T(128)} %constant.101.clone.1, s32[]{:T(128)} %constant.90.clone.1) | dynamic-update-slice | bytes 3141636 | tf_op jit(solution)/shard_map/dynamic_update_slice | solution.py:168
  165.5 4.1 %fusion.80 = (f32[4,1024,128]{1,2,0:T(8,128)S(1)}, f32[4,1024,128]{1,2,0:T(8,128)}) fusion(f32[4,2048,128]{1,2,0:T(8,128)} %dynamic_update_slice.15), kind=kLoop, calls=%fused_computation.137 | loop fusion | bytes 8388608 | tf_op jit(solution)/shard_map/slice | solution.py:190
  173.7 3.1 %convolution_convert_fusion = bf16[4,512,128]{2,1,0:T(8,128)(2,1)S(1)} fusion(bf16[4,512,767]{2,1,0:T(8,128)(2,1)} %copy-done.17, bf16[4,2048,128]{2,1,0:T(8,128)(2,1)} %bitcast.248), kind=kOutput, calls=%fused_computation.69 | convolution fusion | flops 402391040 | bytes 4456448 | tf_op jit(solution)/shard_map/hqk,hkd->hqd/dot_general | solution.py:179
  184.4 3.1 %copy.82 = f32[1024,512]{1,0:T(8,128)} copy(f32[1024,512]{0,1:T(8,128)} %bitcast.225) | data formatting | bytes 4194304 | tf_op jit(solution)/shard_map/reshape | solution.py:85
  187.5 3.2 %fusion.38 = bf16[4,512,128]{2,1,0:T(8,128)(2,1)S(1)} fusion(bf16[4,512,767]{2,1,0:T(8,128)(2,1)} %get-tuple-element.32, f32[4,1024,128]{2,1,0:T(8,128)S(1)} %bitcast.219, bf16[4,2048,128]{2,1,0:T(8,128)(2,1)} %bitcast.244), kind=kOutput, calls=%fused_computation.68 | convolution fusion | flops 402653184 | bytes 5505024 | tf_op jit(solution)/shard_map/hqk,hkd->hqd/dot_general | solution.py:161
  194.9 3.7 %add_convert_fusion.1 = bf16[1024,512]{1,0:T(8,128)(2,1)} fusion(f32[1024,512]{1,0:T(8,128)} %copy.78, f32[1024,512]{1,0:T(8,128)} %collective-permute-done.2), kind=kLoop, calls=%fused_computation.57 | loop fusion | flops 1048576 | bytes 5242880 | tf_op jit(solution)/shard_map/convert_element_type | solution.py:199
  199.4 2.9 %add_convert_fusion = bf16[1024,512]{1,0:T(8,128)(2,1)} fusion(f32[1024,512]{1,0:T(8,128)S(1)} %copy-done.6, f32[1024,512]{1,0:T(8,128)} %collective-permute-done.3), kind=kLoop, calls=%fused_computation.56 | loop fusion | flops 1048576 | bytes 5242880 | tf_op jit(solution)/shard_map/convert_element_type | solution.py:199
  (116 shorter events, 72.5 us)
Async XLA Ops:
  7.2 67.4 %reduce-scatter.2.cloned.1.call-start = ((), (), s32[]{:S(2)}) async-start(), calls=%async_computation.2 | async-start | bytes 5242880 | tf_op jit(solution)/shard_map/reduce_scatter | solution.py:68
  8.8 2.5 %copy-start.2 = (bf16[1,1024,4]{1,2,0:T(4,128)(2,1)S(1)}, bf16[1,1024,4]{1,2,0:T(4,128)(2,1)}, u32[]{:S(2)}) copy-start(bf16[1,1024,4]{1,2,0:T(4,128)(2,1)} %param.28) | copy-start | bytes 24580
  28.6 10.0 %copy-start.20 = (s32[1024]{0:T(1024)S(1)}, s32[1024]{0:T(1024)}, u32[]{:S(2)}) copy-start(s32[1024]{0:T(1024)} %param.23) | copy-start | bytes 12292
  29.2 11.6 %copy-start.9 = (bf16[1024,512]{0,1:T(8,128)(2,1)}, bf16[1024,512]{0,1:T(8,128)(2,1)S(1)}, u32[]{:S(2)}) copy-start(bf16[1024,512]{0,1:T(8,128)(2,1)S(1)} %copy.67) | copy-start | bytes 3145732
  29.2 18.2 %collective-permute-start.1 = (bf16[1024,512]{0,1:T(8,128)(2,1)S(1)}, bf16[1024,512]{0,1:T(8,128)(2,1)}, u32[]{:S(2)}, u32[]{:S(2)}) collective-permute-start(bf16[1024,512]{0,1:T(8,128)(2,1)S(1)} %copy.67), channel_id=1, source_target_pairs={{0,1},{1,4},{4,5},{5,8},{8,9},{9,12},{12,13},{2,3},{3,6},{6,7},{7,... | collective-permute-start | bytes 3145736 | tf_op jit(solution)/shard_map/ppermute | solution.py:15
  35.3 21.5 %collective-permute-start = (bf16[1024,512]{0,1:T(8,128)(2,1)S(1)}, bf16[1024,512]{0,1:T(8,128)(2,1)}, u32[]{:S(2)}, u32[]{:S(2)}) collective-permute-start(bf16[1024,512]{0,1:T(8,128)(2,1)S(1)} %copy.64), channel_id=1, source_target_pairs={{0,1},{1,4},{4,5},{5,8},{8,9},{9,12},{12,13},{2,3},{3,6},{6,7},{7,... | collective-permute-start | bytes 3145736 | tf_op jit(solution)/shard_map/ppermute | solution.py:15
  39.3 2.8 %copy-start.21 = (s32[1024]{0:T(1024)}, s32[1024]{0:T(1024)S(1)}, u32[]{:S(2)}) copy-start(s32[1024]{0:T(1024)S(1)} %iota.20) | copy-start | bytes 12292
  58.2 2.5 %copy-start.10 = (bf16[1024,4,128]{2,0,1:T(8,128)(2,1)S(1)}, bf16[1024,4,128]{2,0,1:T(8,128)(2,1)}, u32[]{:S(2)}) copy-start(bf16[1024,4,128]{2,0,1:T(8,128)(2,1)} %copy.71) | copy-start | bytes 3145732
  76.7 18.3 %all-to-all-start = ((bf16[4,128,512]{2,1,0:T(8,128)(2,1)}), bf16[4,128,512]{2,1,0:T(8,128)(2,1)S(1)}, u32[]{:S(2)}, u32[]{:S(2)}) async-start(bf16[4,128,512]{2,1,0:T(8,128)(2,1)} %bitcast.31), calls=%async_computation.1 | async-start | bytes 1048576 | tf_op jit(solution)/shard_map/all_to_all | solution.py:109
  95.0 4.0 %copy-start.22 = (pred[1024]{0:T(1024)(128)(4,1)S(1)}, pred[1024]{0:T(1024)(128)(4,1)}, u32[]{:S(2)}) copy-start(pred[1024]{0:T(1024)(128)(4,1)} %get-tuple-element.28) | copy-start | bytes 3076
  95.0 4.0 %copy-start.23 = (pred[1024]{0:T(1024)(128)(4,1)S(1)}, pred[1024]{0:T(1024)(128)(4,1)}, u32[]{:S(2)}) copy-start(pred[1024]{0:T(1024)(128)(4,1)} %get-tuple-element.29) | copy-start | bytes 3076
  104.8 6.9 %copy-start.3 = (f32[1024,4,128]{2,0,1:T(8,128)}, f32[1024,4,128]{2,0,1:T(8,128)S(1)}, u32[]{:S(2)}) copy-start(f32[1024,4,128]{2,0,1:T(8,128)S(1)} %copy.61) | copy-start | bytes 6291460
  111.8 11.7 %copy-start.17 = (bf16[4,512,767]{2,1,0:T(8,128)(2,1)}, bf16[4,512,767]{2,1,0:T(8,128)(2,1)S(1)}, u32[]{:S(2)}) copy-start(bf16[4,512,767]{2,1,0:T(8,128)(2,1)S(1)} %fusion.8) | copy-start | bytes 9424900
  111.8 7.2 %copy-start.11 = (bf16[1024,4,128]{2,0,1:T(8,128)(2,1)S(1)}, bf16[1024,4,128]{2,0,1:T(8,128)(2,1)}, u32[]{:S(2)}) copy-start(bf16[1024,4,128]{2,0,1:T(8,128)(2,1)} %copy.71) | copy-start | bytes 3145732
  142.3 52.5 %collective-permute-start.2 = (f32[1024,512]{1,0:T(8,128)}, f32[1024,512]{1,0:T(8,128)}, u32[]{:S(2)}, u32[]{:S(2)}) collective-permute-start(f32[1024,512]{1,0:T(8,128)} %copy.77), channel_id=1, source_target_pairs={{1,0},{4,1},{5,4},{8,5},{9,8},{12,9},{13,12},{3,2},{6,3},{7,6},{10... | collective-permute-start | bytes 6291464 | tf_op jit(solution)/shard_map/ppermute | solution.py:15
  148.7 3.0 %copy-start.4 = (f32[1024,4,128]{2,0,1:T(8,128)S(1)}, f32[1024,4,128]{2,0,1:T(8,128)}, u32[]{:S(2)}) copy-start(f32[1024,4,128]{2,0,1:T(8,128)} %copy-done.3) | copy-start | bytes 6291460
  148.7 4.0 %copy-start.16 = (bf16[4,512,767]{2,1,0:T(8,128)(2,1)S(1)}, bf16[4,512,767]{2,1,0:T(8,128)(2,1)}, u32[]{:S(2)}) copy-start(bf16[4,512,767]{2,1,0:T(8,128)(2,1)} %get-tuple-element.32) | copy-start | bytes 9424900
  171.5 5.3 %copy-start.15 = (bf16[4,512,767]{2,1,0:T(8,128)(2,1)S(1)}, bf16[4,512,767]{2,1,0:T(8,128)(2,1)}, u32[]{:S(2)}) copy-start(bf16[4,512,767]{2,1,0:T(8,128)(2,1)} %copy-done.14) | copy-start | bytes 9424900
  171.5 27.9 %collective-permute-start.3 = (f32[1024,512]{1,0:T(8,128)}, f32[1024,512]{1,0:T(8,128)}, u32[]{:S(2)}, u32[]{:S(2)}) collective-permute-start(f32[1024,512]{1,0:T(8,128)} %copy.81), channel_id=1, source_target_pairs={{1,0},{4,1},{5,4},{8,5},{9,8},{12,9},{13,12},{3,2},{6,3},{7,6},{10... | collective-permute-start | bytes 6291464 | tf_op jit(solution)/shard_map/ppermute | solution.py:15
  179.0 3.6 %copy-start.7 = (f32[4,1024,128]{1,2,0:T(8,128)S(1)}, f32[4,1024,128]{1,2,0:T(8,128)}, u32[]{:S(2)}) copy-start(f32[4,1024,128]{1,2,0:T(8,128)} %get-tuple-element.19) | copy-start | bytes 6291460
  184.4 3.1 %copy-start.5 = (f32[1024,4,128]{2,0,1:T(8,128)S(1)}, f32[1024,4,128]{2,0,1:T(8,128)}, u32[]{:S(2)}) copy-start(f32[1024,4,128]{2,0,1:T(8,128)} %copy-done.3) | copy-start | bytes 6291460
  187.5 3.2 %copy-start.13 = (bf16[4,512,767]{2,1,0:T(8,128)(2,1)S(1)}, bf16[4,512,767]{2,1,0:T(8,128)(2,1)}, u32[]{:S(2)}) copy-start(bf16[4,512,767]{2,1,0:T(8,128)(2,1)} %get-tuple-element.30) | copy-start | bytes 9424900
  194.9 4.5 %copy-start.6 = (f32[1024,512]{1,0:T(8,128)S(1)}, f32[1024,512]{1,0:T(8,128)}, u32[]{:S(2)}) copy-start(f32[1024,512]{1,0:T(8,128)} %copy.82) | copy-start | bytes 6291460
  194.9 7.5 %copy-start.1 = (bf16[1024,1024]{1,0:T(8,128)(2,1)S(1)}, bf16[1024,1024]{1,0:T(8,128)(2,1)}, u32[]{:S(2)}) copy-start(bf16[1024,1024]{1,0:T(8,128)(2,1)} %param.24) | copy-start | bytes 6291460
  (8 other events, 10.9 us)
Sparse Core Ops, SparseCore 0:
  27.5 47.0 reduce-scatter.1
where the time goes:
time: 211 us; the launch traced here: 209 us
  local copies, waits for them, and re-layouts  81 us (38%)
  matrix products  55.6 us (26%)
  waiting for transfers between devices  21.3 us (10%)
  other arithmetic  20 us (9%)
  starting transfers between devices  16.6 us (8%)
  between operations  14.5 us (7%)
    dot_general x2, matrix products, shards(): jnp.einsum('hqd,hkd->hqk', grad_attn, v_part, preferred_element_type=jnp....  14.1 us
    dynamic_update_slice x2, local copies, waits for them, and re-layouts, shards(): lax.dynamic_update_slice_in_dim(grad_values, grad_values[:, low_k:high_k]...  13.9 us
    dynamic_update_slice x2, local copies, waits for them, and re-layouts, shards(): lax.dynamic_update_slice_in_dim(grad_keys, grad_keys[:, low_k:high_k] + k...  13.7 us
    unnamed x56, local copies, waits for them, and re-layouts  13.2 us
    dot_general x2, matrix products, shards(): jnp.einsum('hqd,hkd->hqk', q_part, k_part, preferred_element_type=jnp.flo...  12.5 us
    ppermute x4, starting transfers between devices, shifted(): return lax.ppermute(block, axis, route)  12.3 us
    reshape x5, local copies, waits for them, and re-layouts, head_major(): return rows_array.reshape(n_rows, local_heads, HDIM).transpose(1, 0, 2)  9.64 us
    reshape x4, local copies, waits for them, and re-layouts, row_major(): return heads_array.transpose(1, 0, 2).reshape(n_rows, n_heads * HDIM)  8.67 us
  transfers between devices with their start and end apart: 6, of which 4 were waited for; matrix products, arithmetic and copies ran while one was open for 39% of the time, Pallas kernels for 0%

commit v1 on v0

v1 whole, which is shorter than its diff:
```python
import functools
import math

import jax
import jax.numpy as jnp
from jax import lax
from jax.experimental import pallas as pl
from jax.experimental.pallas import tpu as pltpu
from jax.sharding import PartitionSpec as P

HDIM = 128
MOST = 256
TILE = 256
GATE_ROWS = 16
F32 = jnp.float32
BF16 = jnp.bfloat16
MESH = pl.DeviceIdType.MESH


def dot(a, b, ca, cb):
    return lax.dot_general(a, b, (((ca,), (cb,)), ((), ())), preferred_element_type=F32)


def logistic_of(x):
    return 0.5 * jnp.tanh(0.5 * x) + 0.5


def kernel(
    n_mp, n_seq, n_tasks,
    q_hbm, k_hbm, v_hbm, u_hbm, go_hbm, seg_ref, slot_ref, x_hbm, tg_ref,
    win_hbm, wout_hbm, wg_ref, tower_ref,
    oq, ok, ov, ou,
    q, u, go, kbuf, vbuf, x, win, wout, wg,
    slope_own, eo_own, xs, xr, xo, zs, zr,
    mask, onehot, wts, slopes, att, carry_k, carry_v, lend, back,
    lsem, xsem, wsend, wrecv, hsend, hrecv, xsend, xrecv, zsend, zrecv, bsend, brecv,
):
    seq = lax.axis_index("seq")
    mp = lax.axis_index("mp")
    pipe = lax.axis_index("pipe")
    pos = seq * 2 + pipe
    tok, feat = q.shape
    heads = feat // HDIM
    tiles = tok // TILE
    own_rows = x.shape[0]
    slot = own_rows // n_seq
    chunks = xo.shape[0]
    chunk = own_rows // chunks
    per = chunk // slot

    partner = {"pipe": 1 - pipe}
    after = {"seq": lax.rem(seq + pipe, n_seq), "pipe": 1 - pipe}
    before = {"seq": lax.rem(seq + n_seq - 1 + pipe, n_seq), "pipe": 1 - pipe}
    mp_peer = [lax.rem(mp + d, n_mp) for d in range(n_mp)]
    seq_peer = [lax.rem(seq + e, n_seq) for e in range(n_seq)]

    loads = {}
    todo = [
        ("win", win_hbm.at[0], win.at[0]),
        ("wout", wout_hbm.at[0], wout.at[0]),
        ("q", q_hbm, q),
        ("k", k_hbm, kbuf.at[pl.ds(MOST, tok)]),
        ("v", v_hbm, vbuf.at[pl.ds(MOST, tok)]),
        ("u", u_hbm, u),
        ("go", go_hbm, go),
    ]
    block_start = [
        pl.multiple_of(pipe * own_rows + seq_peer[(i + 1) % n_seq] * slot, slot)
        for i in range(n_seq)
    ]
    x_loads = [
        pltpu.make_async_copy(
            x_hbm.at[pl.ds(block_start[i], slot)], x.at[pl.ds(i * slot, slot)], xsem.at[i]
        )
        for i in range(n_seq)
    ]
    for c in x_loads:
        c.start()
    for i, (name, src, dst) in enumerate(todo):
        loads[name] = pltpu.make_async_copy(src, dst, lsem.at[i])
        loads[name].start()

    barrier = pltpu.get_barrier_semaphore()
    greet = [partner, after, before]
    greet += [{"mp": mp_peer[d]} for d in range(1, n_mp)]
    greet += [{"seq": seq_peer[e]} for e in range(1, n_seq)]
    for who in greet:
        pl.semaphore_signal(barrier, inc=1, device_id=who, device_id_type=MESH)
    pl.semaphore_wait(barrier, len(greet))

    def remote(src, dst, ssem, rsem, who):
        return pltpu.make_async_remote_copy(
            src_ref=src, dst_ref=dst, send_sem=ssem, recv_sem=rsem,
            device_id=who, device_id_type=MESH,
        )

    weights_x = [
        remote(win_hbm.at[0], win.at[1], wsend.at[0], wrecv.at[0], partner),
        remote(wout_hbm.at[0], wout.at[1], wsend.at[1], wrecv.at[1], partner),
        remote(wg_ref, wg.at[pl.ds(GATE_ROWS, GATE_ROWS)], wsend.at[2], wrecv.at[2], partner),
    ]
    for c in weights_x:
        c.start()
    halo_x = [
        remote(k_hbm.at[pl.ds(tok - MOST, MOST)], kbuf.at[pl.ds(0, MOST)],
               hsend.at[0], hrecv.at[0], after),
        remote(v_hbm.at[pl.ds(tok - MOST, MOST)], vbuf.at[pl.ds(0, MOST)],
               hsend.at[1], hrecv.at[1], after),
    ]
    for c in halo_x:
        c.start()

    wg[0:GATE_ROWS, :] = wg_ref[...]
    towers = tower_ref[...].astype(F32)

    def front(rows, e):
        pre = dot(x[rows, :], win[e], 1, 0)
        lg = logistic_of(pre)
        act = (pre * lg).astype(BF16)
        eo = dot(act, wout[e], 1, 0)
        return lg * (1.0 + pre * (1.0 - lg)), eo

    for c in x_loads:
        c.wait()
    loads["win"].wait()
    loads["wout"].wait()

    def own_front(c, _):
        rows = pl.ds(pl.multiple_of(c * chunk, chunk), chunk)
        s, e = front(rows, 0)
        slope_own[rows, :] = s
        eo_own[rows, :] = e
        return 0

    lax.fori_loop(0, chunks, own_front, 0)

    for c in weights_x:
        c.wait_recv()

    x_sends = {}
    lanes = lax.broadcasted_iota(jnp.int32, (chunk, 2 * GATE_ROWS), 1)
    for c in range(chunks):
        rows = pl.ds(c * chunk, chunk)
        tg = jnp.concatenate(
            [tg_ref[pl.ds(block_start[i], slot), :] for i in range(c * per, (c + 1) * per)], axis=0
        )
        gate = logistic_of(dot(x[rows, :], wg[...], 1, 1))
        weighted = tg * gate
        score = jnp.zeros_like(gate)
        slope_p, eo_p = front(rows, 1)
        grad_pre = []
        for e in range(2):
            eo = eo_own[rows, :] if e == 0 else eo_p
            slope = slope_own[rows, :] if e == 0 else slope_p
            hidden = 0.0
            for t in range(n_tasks):
                col = e * GATE_ROWS + t
                got = jnp.sum(eo * towers[t:t + 1, :], axis=1, keepdims=True)
                score = jnp.where(lanes == col, got, score)
                hidden = hidden + weighted[:, col:col + 1] * towers[t:t + 1, :]
            grad_act = dot(hidden.astype(BF16), wout[e], 1, 1)
            grad_pre.append((grad_act * slope).astype(BF16))
        logit = (tg * score * gate * (1.0 - gate)).astype(BF16)
        for d in list(range(1, n_mp)) + [0]:
            cols = pl.ds(pl.multiple_of(mp_peer[d] * feat, feat), feat)
            term = dot(grad_pre[0], win[0, cols, :], 1, 1)
            term = term + dot(grad_pre[1], win[1, cols, :], 1, 1)
            term = term + dot(logit, wg[:, cols], 1, 0)
            if d == 0:
                xo[c] = term
            else:
                xs[c, d - 1] = term.astype(BF16)
                x_sends[c, d] = remote(
                    xs.at[c, d - 1], xr.at[c, d - 1], xsend.at[c, d - 1], xrecv.at[c, d - 1],
                    {"mp": mp_peer[d]},
                )
                x_sends[c, d].start()

    score_scale = 1.0 / math.sqrt(HDIM)
    weight_norm = 1.0 / math.sqrt(MOST)

    seg_here = seg_ref[:, pl.ds(pl.multiple_of(pos * tok, tok), tok)]
    prev_at = pl.multiple_of(jnp.maximum(pos * tok - MOST, 0), MOST)
    seg_prev = jnp.where(pos > 0, seg_ref[:, pl.ds(prev_at, MOST)], -1)
    seg_all = jnp.concatenate([seg_prev, seg_here], axis=1)
    slot_row = slot_ref[...]
    lane128 = lax.broadcasted_iota(jnp.int32, (TILE, HDIM), 1)
    key_at = lax.broadcasted_iota(jnp.int32, (TILE, MOST + TILE), 1) - MOST
    query_at = lax.broadcasted_iota(jnp.int32, (TILE, MOST + TILE), 0)
    causal = key_at <= query_at

    def as_columns(row):
        return jnp.broadcast_to(row, (HDIM, TILE)).T

    def build(i):
        lo = i * TILE
        here = as_columns(seg_all[:, MOST + lo:MOST + lo + TILE])
        here = jnp.concatenate([here] * ((MOST + TILE) // HDIM), axis=1)
        seen = (here == seg_all[:, lo:lo + MOST + TILE]) & causal
        mask[lo:lo + TILE, :] = jnp.where(seen, weight_norm, 0.0)
        want = as_columns(slot_row[:, lo:lo + TILE])
        for b in range(own_rows // HDIM):
            onehot[lo:lo + TILE, b * HDIM:(b + 1) * HDIM] = jnp.where(
                want == lane128 + b * HDIM, 1.0, 0.0
            ).astype(BF16)

    def first_part(i):
        build(i)
        rows = pl.ds(i * TILE, TILE)
        win_rows = pl.ds(i * TILE, MOST + TILE)

        def one(h, _):
            col = pl.ds(pl.multiple_of(h * HDIM, HDIM), HDIM)
            s = dot(q[rows, col], kbuf[win_rows, col], 1, 1) * score_scale
            lg = logistic_of(s)
            sl = s * lg
            m = mask[rows, :]
            w = (sl * m).astype(BF16)
            wts[i, h] = w
            slopes[i, h] = (lg + sl * (1.0 - lg)) * (m * score_scale)
            att[rows, col] = dot(w, vbuf[win_rows, col], 1, 0)
            return 0

        lax.fori_loop(0, heads, one, 0)

    z_sends = {}

    def forward(c):
        total = xo[c]
        for d in range(1, n_mp):
            x_sends[c, d].wait_recv()
            total = total + xr[c, d - 1].astype(F32)
        zs[pl.ds(c * chunk, chunk), :] = total.astype(BF16)
        mine = pl.ds(pl.multiple_of(seq * slot, slot), slot)
        for i in range(c * per, (c + 1) * per):
            part = pl.ds(i * slot, slot)
            if i == n_seq - 1:
                zr[mine, :] = zs[part, :]
            else:
                z_sends[i] = remote(
                    zs.at[part], zr.at[mine], zsend.at[i], zrecv.at[i], {"seq": seq_peer[i + 1]}
                )
                z_sends[i].start()

    loads["q"].wait()
    loads["k"].wait()
    loads["v"].wait()
    for c in halo_x:
        c.wait_recv()
    done = 0
    for i in range(tiles):
        first_part(i)
        while done < chunks and (done + 1) * tiles <= (i + 1) * chunks * 2 - 1:
            forward(done)
            done += 1
    while done < chunks:
        forward(done)
        done += 1
    loads["u"].wait()
    loads["go"].wait()
    for i in range(n_seq - 1):
        z_sends[i].wait_recv()

    def second_part(i):
        rows = pl.ds(i * TILE, TILE)
        win_rows = pl.ds(i * TILE, MOST + TILE)

        def one(h, _):
            col = pl.ds(pl.multiple_of(h * HDIM, HDIM), HDIM)
            qh = q[rows, col]
            kh = kbuf[win_rows, col]
            vh = vbuf[win_rows, col]
            up = go[rows, col].astype(F32) + dot(onehot[rows, :], zr[:, col], 1, 0)
            ou[rows, col] = (up * att[rows, col]).astype(BF16)
            ga = (up * u[rows, col].astype(F32)).astype(BF16)
            gw = dot(ga, vh, 1, 1)
            gs = (gw * slopes[i, h]).astype(BF16)
            gv = dot(wts[i, h], ga, 0, 0)
            gk = dot(gs, qh, 0, 0)
            oq[rows, col] = dot(gs, kh, 1, 0).astype(BF16)
            if i == 0:
                lend[0, :, col] = gk[:MOST].astype(BF16)
                lend[1, :, col] = gv[:MOST].astype(BF16)
            else:
                last = pl.ds((i - 1) * TILE, TILE)
                ok[last, col] = (carry_k[:, col] + gk[:MOST]).astype(BF16)
                ov[last, col] = (carry_v[:, col] + gv[:MOST]).astype(BF16)
            carry_k[:, col] = gk[MOST:]
            carry_v[:, col] = gv[MOST:]
            return 0

        lax.fori_loop(0, heads, one, 0)

    back_x = []
    for i in range(tiles):
        second_part(i)
        if i == 0:
            for j in range(2):
                back_x.append(
                    remote(lend.at[j], back.at[j], bsend.at[j], brecv.at[j], before)
                )
                back_x[j].start()
    last = pl.ds(tok - TILE, TILE)
    back_x[0].wait_recv()
    ok[last, :] = (carry_k[...] + back[0].astype(F32)).astype(BF16)
    back_x[1].wait_recv()
    ov[last, :] = (carry_v[...] + back[1].astype(F32)).astype(BF16)
    for c in weights_x + halo_x + list(x_sends.values()) + list(z_sends.values()) + back_x:
        c.wait_send()


def shards(
    query, key_in, value_in, gate_u, grad_out, segment_ids, sample_slot,
    owned_input, task_grad, w_in, w_out, w_gate, tower,
):
    n_mp = lax.axis_size("mp")
    n_seq = lax.axis_size("seq")
    n_pipe = lax.axis_size("pipe")
    assert n_pipe == 2 and w_in.shape[0] == 1
    tok, feat = query.shape
    heads = feat // HDIM
    tiles = tok // TILE
    own_rows = owned_input.shape[0] // n_pipe
    width = owned_input.shape[1]
    hidden = w_in.shape[2]
    outs = w_out.shape[2]
    n_tasks = w_gate.shape[2]
    chunk = 256
    chunks = own_rows // chunk
    window = MOST + TILE

    gates = jnp.pad(w_gate[0].T, ((0, GATE_ROWS - n_tasks), (0, 0)))
    tg = jnp.pad(task_grad, ((0, 0), (0, GATE_ROWS - n_tasks)))
    tg = jnp.concatenate([tg, tg], axis=1)
    any_spec = pl.BlockSpec(memory_space=pl.ANY)
    vmem_spec = pl.BlockSpec(memory_space=pltpu.VMEM)
    dma = pltpu.SemaphoreType.DMA
    out = jax.ShapeDtypeStruct((tok, feat), BF16)
    return pl.pallas_call(
        functools.partial(kernel, n_mp, n_seq, n_tasks),
        out_shape=(out,) * 4,
        in_specs=[any_spec] * 5 + [vmem_spec] * 2 + [any_spec, vmem_spec]
        + [any_spec] * 2 + [vmem_spec] * 2,
        out_specs=(vmem_spec,) * 4,
        scratch_shapes=[
            pltpu.VMEM((tok, feat), BF16),
            pltpu.VMEM((tok, feat), BF16),
            pltpu.VMEM((tok, feat), BF16),
            pltpu.VMEM((tok + MOST, feat), BF16),
            pltpu.VMEM((tok + MOST, feat), BF16),
            pltpu.VMEM((own_rows, width), BF16),
            pltpu.VMEM((2, width, hidden), BF16),
            pltpu.VMEM((2, hidden, outs), BF16),
            pltpu.VMEM((2 * GATE_ROWS, width), BF16),
            pltpu.VMEM((own_rows, hidden), F32),
            pltpu.VMEM((own_rows, outs), F32),
            pltpu.VMEM((chunks, n_mp - 1, chunk, feat), BF16),
            pltpu.VMEM((chunks, n_mp - 1, chunk, feat), BF16),
            pltpu.VMEM((chunks, chunk, feat), F32),
            pltpu.VMEM((own_rows, feat), BF16),
            pltpu.VMEM((own_rows, feat), BF16),
            pltpu.VMEM((tok, window), F32),
            pltpu.VMEM((tok, own_rows), BF16),
            pltpu.VMEM((tiles, heads, TILE, window), BF16),
            pltpu.VMEM((tiles, heads, TILE, window), F32),
            pltpu.VMEM((tok, feat), F32),
            pltpu.VMEM((MOST, feat), F32),
            pltpu.VMEM((MOST, feat), F32),
            pltpu.VMEM((2, MOST, feat), BF16),
            pltpu.VMEM((2, MOST, feat), BF16),
            dma((7,)),
            dma((n_seq,)),
            dma((3,)),
            dma((3,)),
            dma((2,)),
            dma((2,)),
            dma((chunks, n_mp - 1)),
            dma((chunks, n_mp - 1)),
            dma((n_seq,)),
            dma((n_seq,)),
            dma((2,)),
            dma((2,)),
        ],
        compiler_params=pltpu.CompilerParams(
            collective_id=0, has_side_effects=True, vmem_limit_bytes=50 * 2**20
        ),
        cost_estimate=pl.CostEstimate(
            flops=6 * 2**30, bytes_accessed=16 * 2**20, transcendentals=4 * 2**20
        ),
    )(
        query, key_in, value_in, gate_u, grad_out,
        segment_ids.reshape(1, -1), sample_slot.reshape(1, -1),
        owned_input, tg, w_in, w_out, gates, tower,
    )


def solution(mesh):
    rows = P(("groups", "seq", "pipe"), "mp")
    expert = P(("mp", "pipe"), None, None)
    return jax.shard_map(
        shards,
        mesh=mesh,
        in_specs=(
            rows, rows, rows, rows, rows,
            P("groups"),
            P(("groups", "seq", "pipe")),
            P(("groups", "seq"), None),
            P(("groups", "seq"), None),
            expert, expert, expert,
            P(),
        ),
        out_specs=(rows,) * 4,
        check_vma=False,
    )
```

time: 211 us -> 52.8 us (0.25)
  local copies, waits for them, and re-layouts: 81 us -> 8.58 us
  matrix products: 55.6 us -> 0 us
  Pallas kernels: 0 us -> 42.5 us
  waiting for transfers between devices: 21.3 us -> 0 us
  other arithmetic: 20 us -> 0.01 us
  starting transfers between devices: 16.6 us -> 0 us
  between operations: 14.5 us -> 0.66 us
    dot_general x18 -> x0, matrix products: 55.6 us -> none  [the longest x2 14.1 us: shards(): jnp.einsum('hqd,hkd->hqk', grad_attn, v_part, preferred_element_type=jnp....]
    pallas_call x0 -> x1, Pallas kernels: none -> 42.5 us  [shards(): pl.pallas_call(functools.partial(kernel, n_mp, n_seq, n_tasks), out_shape...]
    dynamic_update_slice x4 -> x0, local copies, waits for them, and re-layouts: 27.7 us -> none  [the longest x2 13.9 us: shards(): lax.dynamic_update_slice_in_dim(grad_values, grad_values[:, low_k:high_k]...]
    reshape x9 -> x0, local copies, waits for them, and re-layouts: 18.3 us -> none  [the longest x5 9.64 us: head_major(): return rows_array.reshape(n_rows, local_heads, HDIM).transpose(1, 0, 2)]
    ppermute x4 -> x0, starting transfers between devices: 12.3 us -> none  [shifted(): return lax.ppermute(block, axis, route)]
    convert_element_type x5 -> x0, other arithmetic: 9.53 us -> none  [the longest x1 3.71 us: shards(): own_keys.astype(jnp.bfloat16)]
    gather x5 -> x0, local copies, waits for them, and re-layouts: 9.16 us -> none  [the longest x1 3.96 us: shards(): jnp.take(flat_rows, jnp.maximum(sample_slot, 0), axis=0).astype(jnp.float32)]
    slice x7 -> x0, local copies, waits for them, and re-layouts: 8.96 us -> none  [the longest x1 4.18 us: shards(): lent_keys = row_major(grad_keys[:, :tok_rows])]
  transfers between devices with their start and end apart: 6 -> 0, of which waited for: 4 -> 0; matrix products, arithmetic and copies ran while one was open for 39% -> 0% of each run, Pallas kernels for 0% -> 0%
where the time goes in v1:
time: 52.8 us; the launch traced here: 51.8 us
  Pallas kernels  42.5 us (80%)
  local copies, waits for them, and re-layouts  8.58 us (16%)
  between operations  0.66 us (1%)
    pallas_call x1, Pallas kernels, shards(): pl.pallas_call(functools.partial(kernel, n_mp, n_seq, n_tasks), out_shape...  42.5 us
    unnamed x14, local copies, waits for them, and re-layouts  6.96 us

profile of v1, /device:TPU:1, one launch (start us, length us, event | category | flops | bytes accessed | tf_op | source)
XLA Modules:
  0.0 51.8 jit_solution(4917402434888693323)
XLA Ops:
  0.6 0.7 %pad.9.wg_ref = bf16[16,1024]{1,0:T(8,128)(2,1)S(1)} pad(bf16[4,1024]{1,0:T(4,128)(2,1)} %bitcast.7, bf16[]{:T(256)} %constant.4.clone.1), padding=0_12x0_0 | pad | bytes 40962 | tf_op jit(solution)/shard_map/jit(_pad)/pad | solution.py:332
  1.3 0.7 %pad.8 = f32[1024,16]{0,1:T(8,128)S(1)} pad(f32[1024,4]{0,1:T(4,128)} %param.21, f32[]{:T(128)} %constant.3.clone.1), padding=0_0x0_12 | pad | bytes 81924 | tf_op jit(solution)/shard_map/jit(_pad)/pad | solution.py:333
  2.1 0.2 copy.18.tg_ref
  2.3 0.0 copy-start
  2.3 0.9 %copy-done = bf16[1,512,256]{2,1,0:T(8,128)(2,1)S(1)} copy-done((bf16[1,512,256]{2,1,0:T(8,128)(2,1)S(1)}, bf16[1,512,256]{2,1,0:T(8,128)(2,1)}, u32[]{:S(2)}) %copy-start) | copy-done | bytes 262168
  3.2 0.0 copy-start.1
  3.2 0.8 %copy-done.1 = s32[8192]{0:T(1024)S(1)} copy-done((s32[8192]{0:T(1024)S(1)}, s32[8192]{0:T(1024)}, u32[]{:S(2)}) %copy-start.1) | copy-done | bytes 32792
  4.0 0.0 copy-start.2
  4.0 0.7 %copy-done.2 = s32[1024]{0:T(1024)S(1)} copy-done((s32[1024]{0:T(1024)S(1)}, s32[1024]{0:T(1024)}, u32[]{:S(2)}) %copy-start.2) | copy-done | bytes 4120
  4.7 0.0 copy-start.3
  4.7 0.7 %copy-done.3 = bf16[4,256]{1,0:T(4,128)(2,1)S(1)} copy-done((bf16[4,256]{1,0:T(4,128)(2,1)S(1)}, bf16[4,256]{1,0:T(4,128)(2,1)}, u32[]{:S(2)}) %copy-start.3) | copy-done | bytes 2072
  5.4 42.5 %shard_map.156 = (bf16[1024,512]{1,0:T(8,128)(2,1)S(1)}, bf16[1024,512]{1,0:T(8,128)(2,1)S(1)}, bf16[1024,512]{1,0:T(8,128)(2,1)S(1)}, bf16[1024,512]{1,0:T(8,128)(2,1)}) custom-call(bf16[1024,512]{1,0:T(8,128)(2,1)} %q_hbm.1, bf16[1024,512]{1,0:T(8,128)(2,1)} %k_hbm.1, bf16[1024,512]{1,0:T(8,128)(2,1)} %v_hbm.1, bf16[1024,512]{1,0:T(8,128)(2,1)} %u_hbm.1, ...), custom_call_target="tpu_custom_call" | custom-call | flops 6442450944 | bytes 16777216 | tf_op jit(solution)/shard_map/pallas_call | solution.py:339
  47.9 1.0 %copy.23 = bf16[1024,512]{1,0:T(8,128)(2,1)} copy(bf16[1024,512]{1,0:T(8,128)(2,1)S(1)} %get-tuple-element.8) | data formatting | bytes 2097152
  48.9 0.0 copy-start.4
  48.9 1.0 %copy.24 = bf16[1024,512]{1,0:T(8,128)(2,1)} copy(bf16[1024,512]{1,0:T(8,128)(2,1)S(1)} %get-tuple-element.9) | data formatting | bytes 2097152
  49.9 1.0 %copy.25 = bf16[1024,512]{1,0:T(8,128)(2,1)} copy(bf16[1024,512]{1,0:T(8,128)(2,1)S(1)} %get-tuple-element.10) | data formatting | bytes 2097152
  50.8 0.0 copy-done.4
  50.8 1.0 %copy.26 = bf16[1024,512]{1,0:T(8,128)(2,1)} copy(bf16[1024,512]{1,0:T(8,128)(2,1)S(1)} %copy-done.4) | data formatting | bytes 2097152
  (1 shorter events, 0.0 us)
Async XLA Ops:
  2.3 1.0 %copy-start = (bf16[1,512,256]{2,1,0:T(8,128)(2,1)S(1)}, bf16[1,512,256]{2,1,0:T(8,128)(2,1)}, u32[]{:S(2)}) copy-start(bf16[1,512,256]{2,1,0:T(8,128)(2,1)} %wout_hbm.1) | copy-start | bytes 786436
  3.2 0.8 %copy-start.1 = (s32[8192]{0:T(1024)S(1)}, s32[8192]{0:T(1024)}, u32[]{:S(2)}) copy-start(s32[8192]{0:T(1024)} %param.18) | copy-start | bytes 98308
  4.0 0.7 %copy-start.2 = (s32[1024]{0:T(1024)S(1)}, s32[1024]{0:T(1024)}, u32[]{:S(2)}) copy-start(s32[1024]{0:T(1024)} %param.19) | copy-start | bytes 12292
  4.7 0.7 %copy-start.3 = (bf16[4,256]{1,0:T(4,128)(2,1)S(1)}, bf16[4,256]{1,0:T(4,128)(2,1)}, u32[]{:S(2)}) copy-start(bf16[4,256]{1,0:T(4,128)(2,1)} %tower_ref.1) | copy-start | bytes 6148
  48.9 1.9 %copy-start.4 = (bf16[1024,512]{1,0:T(8,128)(2,1)S(1)}, bf16[1024,512]{1,0:T(8,128)(2,1)}, u32[]{:S(2)}) copy-start(bf16[1024,512]{1,0:T(8,128)(2,1)} %get-tuple-element.11) | copy-start | bytes 3145732

commit v2 on v1

--- a/solution.py
+++ b/solution.py
@@ -27,13 +27,14 @@
 
 def kernel(
     n_mp, n_seq, n_tasks,
-    q_hbm, k_hbm, v_hbm, u_hbm, go_hbm, seg_ref, slot_ref, x_hbm, tg_ref,
-    win_hbm, wout_hbm, wg_ref, tower_ref,
-    oq, ok, ov, ou,
+    q_hbm, k_hbm, v_hbm, u_hbm, go_hbm, seg_hbm, slot_hbm, x_hbm, tg_hbm,
+    win_hbm, wout_hbm, gate_hbm, tower_hbm,
+    oq_hbm, ok_hbm, ov_hbm, ou_hbm,
+    oq, ok, ov, ou, seg_ref, slot_ref, tg_in, gate_in, tower_ref, tg_wide, tg_ref,
     q, u, go, kbuf, vbuf, x, win, wout, wg,
     slope_own, eo_own, xs, xr, xo, zs, zr,
     mask, onehot, wts, slopes, att, carry_k, carry_v, lend, back,
-    lsem, xsem, wsend, wrecv, hsend, hrecv, xsend, xrecv, zsend, zrecv, bsend, brecv,
+    lsem, xsem, wsend, wrecv, hsend, hrecv, xsend, xrecv, zsend, zrecv, bsend, brecv, osem,
 ):
     seq = lax.axis_index("seq")
     mp = lax.axis_index("mp")
@@ -58,6 +59,11 @@
     todo = [
         ("win", win_hbm.at[0], win.at[0]),
         ("wout", wout_hbm.at[0], wout.at[0]),
+        ("gate", gate_hbm, gate_in),
+        ("tg", tg_hbm, tg_in),
+        ("tower", tower_hbm, tower_ref),
+        ("seg", seg_hbm, seg_ref),
+        ("slot", slot_hbm, slot_ref),
         ("q", q_hbm, q),
         ("k", k_hbm, kbuf.at[pl.ds(MOST, tok)]),
         ("v", v_hbm, vbuf.at[pl.ds(MOST, tok)]),
@@ -68,6 +74,7 @@
         pl.multiple_of(pipe * own_rows + seq_peer[(i + 1) % n_seq] * slot, slot)
         for i in range(n_seq)
     ]
+    block_at = [pl.multiple_of(seq_peer[(i + 1) % n_seq] * slot, slot) for i in range(n_seq)]
     x_loads = [
         pltpu.make_async_copy(
             x_hbm.at[pl.ds(block_start[i], slot)], x.at[pl.ds(i * slot, slot)], xsem.at[i]
@@ -79,6 +86,11 @@
     for i, (name, src, dst) in enumerate(todo):
         loads[name] = pltpu.make_async_copy(src, dst, lsem.at[i])
         loads[name].start()
+
+    tg_wide[...] = jnp.zeros_like(tg_wide)
+    loads["gate"].wait()
+    tg_wide[0:n_tasks, 0:gate_in.shape[1]] = gate_in[...].astype(F32)
+    wg[0:GATE_ROWS, :] = tg_wide[0:GATE_ROWS, 0:gate_in.shape[1]].astype(BF16)
 
     barrier = pltpu.get_barrier_semaphore()
     greet = [partner, after, before]
@@ -97,7 +109,7 @@
     weights_x = [
         remote(win_hbm.at[0], win.at[1], wsend.at[0], wrecv.at[0], partner),
         remote(wout_hbm.at[0], wout.at[1], wsend.at[1], wrecv.at[1], partner),
-        remote(wg_ref, wg.at[pl.ds(GATE_ROWS, GATE_ROWS)], wsend.at[2], wrecv.at[2], partner),
+        remote(wg.at[pl.ds(0, GATE_ROWS)], wg.at[pl.ds(GATE_ROWS, GATE_ROWS)], wsend.at[2], wrecv.at[2], partner),
     ]
     for c in weights_x:
         c.start()
@@ -110,7 +122,12 @@
     for c in halo_x:
         c.start()
 
-    wg[0:GATE_ROWS, :] = wg_ref[...]
+    loads["tg"].wait()
+    loads["tower"].wait()
+    half = tg_in[:, pl.ds(pl.multiple_of(pipe * own_rows, own_rows), own_rows)]
+    tg_wide[0:n_tasks, 0:own_rows] = half
+    tg_wide[GATE_ROWS:GATE_ROWS + n_tasks, 0:own_rows] = half
+    tg_ref[...] = tg_wide[:, 0:own_rows].T
     towers = tower_ref[...].astype(F32)
 
     def front(rows, e):
@@ -142,7 +159,7 @@
     for c in range(chunks):
         rows = pl.ds(c * chunk, chunk)
         tg = jnp.concatenate(
-            [tg_ref[pl.ds(block_start[i], slot), :] for i in range(c * per, (c + 1) * per)], axis=0
+            [tg_ref[pl.ds(block_at[i], slot), 0:2 * GATE_ROWS] for i in range(c * per, (c + 1) * per)], axis=0
         )
         gate = logistic_of(dot(x[rows, :], wg[...], 1, 1))
         weighted = tg * gate
@@ -179,6 +196,8 @@
     score_scale = 1.0 / math.sqrt(HDIM)
     weight_norm = 1.0 / math.sqrt(MOST)
 
+    loads["seg"].wait()
+    loads["slot"].wait()
     seg_here = seg_ref[:, pl.ds(pl.multiple_of(pos * tok, tok), tok)]
     prev_at = pl.multiple_of(jnp.maximum(pos * tok - MOST, 0), MOST)
     seg_prev = jnp.where(pos > 0, seg_ref[:, pl.ds(prev_at, MOST)], -1)
@@ -216,12 +235,12 @@
             sl = s * lg
             m = mask[rows, :]
             w = (sl * m).astype(BF16)
-            wts[i, h] = w
+            wts[i, h] = w.T
             slopes[i, h] = (lg + sl * (1.0 - lg)) * (m * score_scale)
             att[rows, col] = dot(w, vbuf[win_rows, col], 1, 0)
             return 0
 
-        lax.fori_loop(0, heads, one, 0)
+        lax.fori_loop(0, heads, one, 0, unroll=True)
 
     z_sends = {}
 
@@ -247,10 +266,11 @@
     loads["v"].wait()
     for c in halo_x:
         c.wait_recv()
-    done = 0
+    forward(0)
+    done = 1
     for i in range(tiles):
         first_part(i)
-        while done < chunks and (done + 1) * tiles <= (i + 1) * chunks * 2 - 1:
+        if done < chunks - 1:
             forward(done)
             done += 1
     while done < chunks:
@@ -275,7 +295,7 @@
             ga = (up * u[rows, col].astype(F32)).astype(BF16)
             gw = dot(ga, vh, 1, 1)
             gs = (gw * slopes[i, h]).astype(BF16)
-            gv = dot(wts[i, h], ga, 0, 0)
+            gv = dot(wts[i, h], ga, 1, 0)
             gk = dot(gs, qh, 0, 0)
             oq[rows, col] = dot(gs, kh, 1, 0).astype(BF16)
             if i == 0:
@@ -289,11 +309,24 @@
             carry_v[:, col] = gv[MOST:]
             return 0
 
-        lax.fori_loop(0, heads, one, 0)
+        lax.fori_loop(0, heads, one, 0, unroll=True)
 
     back_x = []
+    stores = []
+
+    def store(ref, hbm, i):
+        rows = pl.ds(i * TILE, TILE)
+        c = pltpu.make_async_copy(ref.at[rows], hbm.at[rows], osem.at[len(stores)])
+        c.start()
+        stores.append(c)
+
     for i in range(tiles):
         second_part(i)
+        store(oq, oq_hbm, i)
+        store(ou, ou_hbm, i)
+        if i > 0:
+            store(ok, ok_hbm, i - 1)
+            store(ov, ov_hbm, i - 1)
         if i == 0:
             for j in range(2):
                 back_x.append(
@@ -303,10 +336,26 @@
     last = pl.ds(tok - TILE, TILE)
     back_x[0].wait_recv()
     ok[last, :] = (carry_k[...] + back[0].astype(F32)).astype(BF16)
+    store(ok, ok_hbm, tiles - 1)
     back_x[1].wait_recv()
     ov[last, :] = (carry_v[...] + back[1].astype(F32)).astype(BF16)
+    store(ov, ov_hbm, tiles - 1)
+    for c in stores:
+        c.wait()
     for c in weights_x + halo_x + list(x_sends.values()) + list(z_sends.values()) + back_x:
         c.wait_send()
+
+
+def settle(*refs):
+    count = (len(refs) - 1) // 2
+    sems = refs[-1]
+    copies = [
+        pltpu.make_async_copy(refs[i], refs[count + i], sems.at[i]) for i in range(count)
+    ]
+    for c in copies:
+        c.start()
+    for c in copies:
+        c.wait()
 
 
 def shards(
@@ -325,24 +374,30 @@
     hidden = w_in.shape[2]
     outs = w_out.shape[2]
     n_tasks = w_gate.shape[2]
-    chunk = 256
+    chunk = 128
     chunks = own_rows // chunk
     window = MOST + TILE
 
-    gates = jnp.pad(w_gate[0].T, ((0, GATE_ROWS - n_tasks), (0, 0)))
-    tg = jnp.pad(task_grad, ((0, 0), (0, GATE_ROWS - n_tasks)))
-    tg = jnp.concatenate([tg, tg], axis=1)
     any_spec = pl.BlockSpec(memory_space=pl.ANY)
-    vmem_spec = pl.BlockSpec(memory_space=pltpu.VMEM)
     dma = pltpu.SemaphoreType.DMA
     out = jax.ShapeDtypeStruct((tok, feat), BF16)
-    return pl.pallas_call(
+    results = pl.pallas_call(
         functools.partial(kernel, n_mp, n_seq, n_tasks),
         out_shape=(out,) * 4,
-        in_specs=[any_spec] * 5 + [vmem_spec] * 2 + [any_spec, vmem_spec]
-        + [any_spec] * 2 + [vmem_spec] * 2,
-        out_specs=(vmem_spec,) * 4,
+        in_specs=[any_spec] * 13,
+        out_specs=(any_spec,) * 4,
         scratch_shapes=[
+            pltpu.VMEM((tok, feat), BF16),
+            pltpu.VMEM((tok, feat), BF16),
+            pltpu.VMEM((tok, feat), BF16),
+            pltpu.VMEM((tok, feat), BF16),
+            pltpu.VMEM((1, segment_ids.shape[0]), jnp.int32),
+            pltpu.VMEM((1, tok), jnp.int32),
+            pltpu.VMEM((n_tasks, owned_input.shape[0]), F32),
+            pltpu.VMEM((n_tasks, width), BF16),
+            pltpu.VMEM((n_tasks, outs), BF16),
+            pltpu.VMEM((HDIM, max(own_rows, width)), F32),
+            pltpu.VMEM((own_rows, HDIM), F32),
             pltpu.VMEM((tok, feat), BF16),
             pltpu.VMEM((tok, feat), BF16),
             pltpu.VMEM((tok, feat), BF16),
@@ -361,14 +416,14 @@
             pltpu.VMEM((own_rows, feat), BF16),
             pltpu.VMEM((tok, window), F32),
             pltpu.VMEM((tok, own_rows), BF16),
-            pltpu.VMEM((tiles, heads, TILE, window), BF16),
+            pltpu.VMEM((tiles, heads, window, TILE), BF16),
             pltpu.VMEM((tiles, heads, TILE, window), F32),
             pltpu.VMEM((tok, feat), F32),
             pltpu.VMEM((MOST, feat), F32),
             pltpu.VMEM((MOST, feat), F32),
             pltpu.VMEM((2, MOST, feat), BF16),
             pltpu.VMEM((2, MOST, feat), BF16),
-            dma((7,)),
+            dma((12,)),
             dma((n_seq,)),
             dma((3,)),
             dma((3,)),
@@ -380,9 +435,10 @@
             dma((n_seq,)),
             dma((2,)),
             dma((2,)),
+            dma((4 * tiles,)),
         ],
         compiler_params=pltpu.CompilerParams(
-            collective_id=0, has_side_effects=True, vmem_limit_bytes=50 * 2**20
+            collective_id=0, has_side_effects=True, vmem_limit_bytes=60 * 2**20
         ),
         cost_estimate=pl.CostEstimate(
             flops=6 * 2**30, bytes_accessed=16 * 2**20, transcendentals=4 * 2**20
@@ -390,8 +446,17 @@
     )(
         query, key_in, value_in, gate_u, grad_out,
         segment_ids.reshape(1, -1), sample_slot.reshape(1, -1),
-        owned_input, tg, w_in, w_out, gates, tower,
+        owned_input, task_grad.T, w_in, w_out, w_gate[0].T, tower,
     )
+    return pl.pallas_call(
+        settle,
+        out_shape=(out,) * 4,
+        in_specs=[any_spec] * 4,
+        out_specs=(any_spec,) * 4,
+        scratch_shapes=[dma((4,))],
+        compiler_params=pltpu.CompilerParams(vmem_limit_bytes=60 * 2**20),
+        cost_estimate=pl.CostEstimate(flops=0, bytes_accessed=8 * 2**20, transcendentals=0),
+    )(*results)
 
 
 def solution(mesh):

time: 52.8 us -> 169 us (3.20)
  Pallas kernels: 42.5 us -> 168 us
  local copies, waits for them, and re-layouts: 8.58 us -> 0 us
    pallas_call x0 -> x1, Pallas kernels: none -> 128 us  [shards(): pl.pallas_call(settle, out_shape=(out,) * 4, in_specs=[any_spec] * 4, out...]
    unnamed x14 -> x0, local copies, waits for them, and re-layouts: 6.96 us -> none
    pallas_call x1, Pallas kernels: 42.5 us -> 40.2 us  [shards(): pl.pallas_call(functools.partial(kernel, n_mp, n_seq, n_tasks), out_shape...]
where the time goes in v2:
time: 169 us
  Pallas kernels  168 us (99%)
    pallas_call x1, Pallas kernels, shards(): pl.pallas_call(settle, out_shape=(out,) * 4, in_specs=[any_spec] * 4, out...  128 us
    pallas_call x1, Pallas kernels, shards(): pl.pallas_call(functools.partial(kernel, n_mp, n_seq, n_tasks), out_shape...  40.2 us

profile of v2, /device:TPU:1, one launch (start us, length us, event | category | flops | bytes accessed | tf_op | source)
XLA Modules:
  0.0 169.2 jit_solution(15557092058033703926)
XLA Ops:
  0.6 40.2 %shard_map.156 = (bf16[1024,512]{1,0:T(8,128)(2,1)}, bf16[1024,512]{1,0:T(8,128)(2,1)}, bf16[1024,512]{1,0:T(8,128)(2,1)}, bf16[1024,512]{1,0:T(8,128)(2,1)}) custom-call(bf16[1024,512]{1,0:T(8,128)(2,1)} %q_hbm.1, bf16[1024,512]{1,0:T(8,128)(2,1)} %k_hbm.1, bf16[1024,512]{1,0:T(8,128)(2,1)} %v_hbm.1, bf16[1024,512]{1,0:T(8,128)(2,1)} %u_hbm.1, ...), custom_call_target="tpu_custom_call" | custom-call | flops 6442450944 | bytes 16777216 | tf_op jit(solution)/shard_map/pallas_call | solution.py:384
  40.8 128.2 %shard_map.157 = (bf16[1024,512]{1,0:T(8,128)(2,1)}, bf16[1024,512]{1,0:T(8,128)(2,1)}, bf16[1024,512]{1,0:T(8,128)(2,1)}, bf16[1024,512]{1,0:T(8,128)(2,1)}) custom-call(bf16[1024,512]{1,0:T(8,128)(2,1)} %get-tuple-element.8.refs_0_, bf16[1024,512]{1,0:T(8,128)(2,1)} %get-tuple-element.9.refs_1_, bf16[1024,512]{1,0:T(8,128)(2,1)} %get-tuple-element.10.refs_2_, ...), custom_call_target="tpu_custom_call" | custom-call | bytes 8388608 | tf_op jit(solution)/shard_map/pallas_call | solution.py:451

commit v3 on v2

--- a/solution.py
+++ b/solution.py
@@ -347,14 +347,25 @@
 
 
 def settle(*refs):
-    count = (len(refs) - 1) // 2
-    sems = refs[-1]
-    copies = [
-        pltpu.make_async_copy(refs[i], refs[count + i], sems.at[i]) for i in range(count)
-    ]
-    for c in copies:
+    count = (len(refs) - 3) // 2
+    held, load_sem, store_sem = refs[-3:]
+    parts = load_sem.shape[1]
+    rows = held.shape[1] // parts
+    every = [(i, pl.ds(j * rows, rows), j) for j in range(parts) for i in range(count)]
+    loads = [
+        pltpu.make_async_copy(refs[i].at[part], held.at[i, part], load_sem.at[i, j])
+        for i, part, j in every
+    ]
+    stores = [
+        pltpu.make_async_copy(held.at[i, part], refs[count + i].at[part], store_sem.at[i, j])
+        for i, part, j in every
+    ]
+    for c in loads:
         c.start()
-    for c in copies:
+    for load, store in zip(loads, stores):
+        load.wait()
+        store.start()
+    for c in stores:
         c.wait()
 
 
@@ -453,7 +464,7 @@
         out_shape=(out,) * 4,
         in_specs=[any_spec] * 4,
         out_specs=(any_spec,) * 4,
-        scratch_shapes=[dma((4,))],
+        scratch_shapes=[pltpu.VMEM((4, tok, feat), BF16), dma((4, 2)), dma((4, 2))],
         compiler_params=pltpu.CompilerParams(vmem_limit_bytes=60 * 2**20),
         cost_estimate=pl.CostEstimate(flops=0, bytes_accessed=8 * 2**20, transcendentals=0),
     )(*results)

time: 169 us -> 44.7 us (0.26)
  Pallas kernels: 168 us -> 43.8 us
    pallas_call x1, Pallas kernels: 128 us -> 3.58 us  [shards(): pl.pallas_call(settle, out_shape=(out,) * 4, in_specs=[any_spec] * 4, out...]
where the time goes in v3:
time: 44.7 us; the launch traced here: 44.6 us
  Pallas kernels  43.8 us (98%)
  between operations  0.8 us (2%)
    pallas_call x1, Pallas kernels, shards(): pl.pallas_call(functools.partial(kernel, n_mp, n_seq, n_tasks), out_shape...  40.2 us
    pallas_call x1, Pallas kernels, shards(): pl.pallas_call(settle, out_shape=(out,) * 4, in_specs=[any_spec] * 4, out...  3.58 us

profile of v3, /device:TPU:1, one launch (start us, length us, event | category | flops | bytes accessed | tf_op | source)
XLA Modules:
  0.0 44.6 jit_solution(3488212430375803288)
XLA Ops:
  0.6 40.2 %shard_map.156 = (bf16[1024,512]{1,0:T(8,128)(2,1)}, bf16[1024,512]{1,0:T(8,128)(2,1)}, bf16[1024,512]{1,0:T(8,128)(2,1)}, bf16[1024,512]{1,0:T(8,128)(2,1)}) custom-call(bf16[1024,512]{1,0:T(8,128)(2,1)} %q_hbm.1, bf16[1024,512]{1,0:T(8,128)(2,1)} %k_hbm.1, bf16[1024,512]{1,0:T(8,128)(2,1)} %v_hbm.1, bf16[1024,512]{1,0:T(8,128)(2,1)} %u_hbm.1, ...), custom_call_target="tpu_custom_call" | custom-call | flops 6442450944 | bytes 16777216 | tf_op jit(solution)/shard_map/pallas_call | solution.py:395
  40.8 3.6 %shard_map.157 = (bf16[1024,512]{1,0:T(8,128)(2,1)}, bf16[1024,512]{1,0:T(8,128)(2,1)}, bf16[1024,512]{1,0:T(8,128)(2,1)}, bf16[1024,512]{1,0:T(8,128)(2,1)}) custom-call(bf16[1024,512]{1,0:T(8,128)(2,1)} %get-tuple-element.8.refs_0_, bf16[1024,512]{1,0:T(8,128)(2,1)} %get-tuple-element.9.refs_1_, bf16[1024,512]{1,0:T(8,128)(2,1)} %get-tuple-element.10.refs_2_, ...), custom_call_target="tpu_custom_call" | custom-call | bytes 8388608 | tf_op jit(solution)/shard_map/pallas_call | solution.py:462
